TPU v7x, 32 devices: a whole 2x2x4 slice. The times are simulated.
32 devices in a mesh: ep: 16 (over z, y, core), dp: 2 (over x).
Axes of the slice: x: 2, y: 2, z: 4, core: 2. Of those that a mesh axis runs over, the one named last changes fastest.
Arguments:
- tokens: bfloat16 [2, 128, 3584], P(None, ('ep', 'dp')), may hold values from -6 to 6
- routing: int32 [2, 128, 8], P(None, 'ep'), may hold values from 0 to 15, all different within a row; in each aligned block of 8 rows (0 to 7, 8 to 15, ..., all dimensions but the last counted through in order) at most 8 rows name the same one
- gate_values: float32 [2, 128, 8], P(None, 'ep'), may hold values from 0.05 to 0.5
- held_weight: bfloat16 [16, 3584, 1024], P('ep', None, 'dp'), may hold values from -0.09375 to 0.09375
- scale_table: float32 [16, 28, 8], P(None, None, 'dp'), may hold values from 0.25 to 4
- old_expert: int32 [16], replicated, may hold values from 0 to 15, as said below
- new_expert: int32 [16], replicated, may hold values from 0 to 15, as said below
Outputs:
- combined: bfloat16 [2, 128, 1024], P(None, 'ep', 'dp')
- moved_weight: bfloat16 [16, 3584, 1024], P('ep', None, 'dp')
Inputs may be any that keep to these rules, and one draw needn't show every extreme that they name: `routing`: each row names 8 different experts; in each aligned block of 8 token rows of a step no expert is named by more than 8 rows. `old_expert`: A permutation of the experts over the slots. `new_expert`: A permutation of the experts over the slots; it equals old_expert except at exactly 4 slots, whose experts are permuted among themselves so that each of them changes.
All inputs are finite; a program needn't handle non-finite values.
Results may differ from a plain program's by a relative error of at most 0.0039.
Values may be sent and summed in bfloat16 or wider, within the bound.
A program may use at most 64 MiB of HBM per device.

v0:
```python
import jax
import jax.numpy as jnp
from jax import lax
from jax.sharding import PartitionSpec as P


def inverse_place(expert_at):
    count = expert_at.shape[0]
    labels = jnp.arange(count, dtype=jnp.int32)
    match = expert_at[None, :] == labels[:, None]
    return jnp.sum(jnp.where(match, labels[None, :], 0), axis=1)


def source_slots(old_expert, new_expert):
    labels = jnp.arange(old_expert.shape[0], dtype=jnp.int32)
    match = old_expert[None, :] == new_expert[:, None]
    return jnp.sum(jnp.where(match, labels[None, :], 0), axis=1)


def scaled_product(token_rows, weight_block, scales):
    row_blocks = scales.shape[0]
    block_rows = weight_block.shape[0] // row_blocks
    partial_value = jnp.einsum(
        "rbi,bif->rbf",
        token_rows.reshape(token_rows.shape[0], row_blocks, block_rows),
        weight_block.reshape(row_blocks, block_rows, weight_block.shape[1]),
        preferred_element_type=jnp.float32,
    )
    widened = jnp.repeat(scales, weight_block.shape[1] // scales.shape[1], axis=1)
    return jnp.sum(partial_value * widened[None, :, :], axis=1)


def expert_service(weight_block, scales):

    def serve_rows(arrived):

        def one_slot(slot_rows):
            return jax.nn.silu(scaled_product(slot_rows, weight_block, scales)).astype(jnp.bfloat16)

        activated = lax.map(one_slot, arrived)
        return lax.all_to_all(activated, "ep", split_axis=1, concat_axis=1, tiled=True)

    return serve_rows


def route_pairs(routing, expert_at, peers):
    pair_ids = routing.reshape(-1)
    labels = jnp.arange(peers, dtype=jnp.int32)
    onehot = (pair_ids[:, None] == labels[None, :]).astype(jnp.int32)
    before = jnp.cumsum(onehot, axis=0) - onehot
    slot_rank = jnp.sum(before * onehot, axis=1)
    owners = jnp.sum(onehot * inverse_place(expert_at)[None, :], axis=1)
    return slot_rank * peers + owners


def shards(tokens, routing, gate_values, held_weight, scale_table, old_expert, new_expert):
    peers = lax.axis_size("ep")
    my_slot = lax.axis_index("ep")
    group_size = routing.shape[1]
    top_count = routing.shape[2]
    capacity = min(group_size, max(2, 2 * group_size * top_count // peers))
    hidden_width = held_weight.shape[2]
    old_block = held_weight[0]
    sources = source_slots(old_expert, new_expert)
    pieces = old_block.reshape(peers, old_block.shape[0] // peers, hidden_width)
    new_block = lax.all_to_all(
        jnp.take(
            lax.all_to_all(pieces, "ep", split_axis=0, concat_axis=0, tiled=True), sources, axis=0
        ),
        "ep",
        split_axis=0,
        concat_axis=0,
        tiled=True,
    ).reshape(old_block.shape)
    first_serve = (new_block, new_expert)
    serve_plans = [first_serve] + [(new_block, new_expert)] * (tokens.shape[0] - 1)
    grouped = lax.all_gather(tokens, "dp", axis=1, tiled=True)
    columns = grouped.shape[2]
    combined_steps = []
    for decode_step in range(tokens.shape[0]):
        weight_block, expert_at = serve_plans[decode_step]
        scales = scale_table[expert_at[my_slot]]
        target = route_pairs(routing[decode_step], expert_at, peers)
        repeated = jnp.repeat(grouped[decode_step], top_count, axis=0)
        send_buffer = jnp.zeros((capacity * peers, columns), grouped.dtype).at[target].set(repeated)
        send_buffer = send_buffer.reshape(capacity, peers, columns)
        serve_rows = expert_service(weight_block, scales)
        returned = serve_rows(
            lax.all_to_all(send_buffer, "ep", split_axis=1, concat_axis=1, tiled=True)
        )
        activated = returned.reshape(capacity * peers, hidden_width)[target].astype(jnp.float32)
        activated = activated.reshape(group_size, top_count, hidden_width)
        weighted = jnp.sum(gate_values[decode_step][:, :, None] * activated, axis=1)
        combined_steps.append(weighted.astype(jnp.bfloat16))
    return (jnp.stack(combined_steps), new_block[None])


def solution(mesh):
    placed = (
        P(None, ("ep", "dp"), None),
        P(None, "ep", None),
        P(None, "ep", None),
        P("ep", None, "dp"),
        P(None, None, "dp"),
        P(),
        P(),
    )
    return jax.shard_map(
        shards,
        mesh=mesh,
        in_specs=placed,
        out_specs=(P(None, "ep", "dp"), P("ep", None, "dp")),
        check_vma=False,
    )
```

profile of v0, /device:TPU:1, one launch (start us, length us, event | category | flops | bytes accessed | tf_op | source)
XLA Modules:
  0.0 311.3 jit_solution(14134027861554811198)
XLA Ops:
  0.6 0.7 fusion.30
  1.7 0.1 reduce_window_sum.17
  1.8 0.1 reduce_window_sum.18
  1.9 0.9 copy.43
  2.7 4.3 %all_gather.3 = bf16[2,8,3584]{2,0,1:T(2,128)(2,1)S(1)} all-gather(bf16[2,4,3584]{2,0,1:T(2,128)(2,1)S(1)} %copy.43), channel_id=1, replica_groups=mesh['ep'=16,'dp'=2] {'dp'}, dimensions={1}, use_global_device_ids=true | all-gather | bytes 172032 | tf_op jit(solution)/shard_map/all_gather | solution.py:77
  7.0 0.2 fusion.29
  7.2 0.9 select_reduce_fusion.4
  8.1 0.2 select_reduce_fusion.3
  8.3 1.5 scatter_custom_fusion.1
  9.9 0.5 copy.51
  10.4 30.7 %all_to_all.30 = bf16[8,16,3584]{2,0,1:T(8,128)(2,1)S(1)} all-to-all(bf16[8,16,3584]{2,0,1:T(8,128)(2,1)S(1)} %copy.51), channel_id=1, replica_groups=mesh['ep'=16,'dp'=2] {'ep'}, dimensions={1} | all-to-all | bytes 1835008 | tf_op jit(solution)/shard_map/all_to_all | solution.py:89
  41.0 4.4 %all-to-all-start.1 = ((bf16[16,224,512]{2,1,0:T(8,128)(2,1)}), bf16[16,224,512]{2,1,0:T(8,128)(2,1)}, u32[]{:S(2)}, u32[]{:S(2)}) async-start(bf16[16,224,512]{2,1,0:T(8,128)(2,1)} %bitcast.113), calls=%async_computation.1 | async-start | bytes 7340032 | tf_op jit(solution)/shard_map/all_to_all | solution.py:68
  45.5 1.5 scatter_custom_fusion
  47.0 1.4 copy.45
  48.5 65.7 %all-to-all-done.1 = bf16[16,224,512]{2,1,0:T(8,128)(2,1)} async-done(((bf16[16,224,512]{2,1,0:T(8,128)(2,1)}), bf16[16,224,512]{2,1,0:T(8,128)(2,1)}, u32[]{:S(2)}, u32[]{:S(2)}) %all-to-all-start.1) | async-done | bytes 3670048 | tf_op jit(solution)/shard_map/all_to_all | solution.py:68
  114.1 17.2 %all-to-all-start = ((bf16[8,16,3584]{2,0,1:T(8,128)(2,1)}), bf16[8,16,3584]{2,0,1:T(8,128)(2,1)S(1)}, u32[]{:S(2)}, u32[]{:S(2)}) async-start(bf16[8,16,3584]{2,0,1:T(8,128)(2,1)} %copy.45), calls=%async_computation | async-start | bytes 1835008 | tf_op jit(solution)/shard_map/all_to_all | solution.py:89
  131.4 4.7 %gather_fusion = bf16[16,224,512]{2,1,0:T(8,128)(2,1)} fusion(bf16[16,224,512]{2,1,0:T(8,128)(2,1)} %all-to-all-done.1, s32[1024]{0:T(1024)S(1)} %pad_clamp_fusion.2), kind=kCustom, calls=%fused_computation | custom fusion | bytes 7340096 | tf_op jit(solution)/shard_map/jit(_take)/gather | solution.py:67
  136.0 4.3 %broadcast_select_fusion = bf16[16,224,512]{2,1,0:T(8,128)(2,1)} fusion(bf16[16,224,512]{2,1,0:T(8,128)(2,1)} %gather_fusion, pred[16]{0:T(512)(128)(4,1)S(1)} %compare_and_fusion), kind=kLoop, calls=%fused_computation.27 | loop fusion | flops 1835008 | bytes 7340048 | tf_op jit(solution)/shard_map/jit(_take)/select_n | solution.py:67
  140.3 11.8 %all-to-all-done = bf16[8,16,3584]{2,0,1:T(8,128)(2,1)S(1)} async-done(((bf16[8,16,3584]{2,0,1:T(8,128)(2,1)}), bf16[8,16,3584]{2,0,1:T(8,128)(2,1)S(1)}, u32[]{:S(2)}, u32[]{:S(2)}) %all-to-all-start) | async-done | bytes 917536 | tf_op jit(solution)/shard_map/all_to_all | solution.py:89
  152.2 6.2 %all-to-all-start.2 = ((bf16[16,224,512]{2,1,0:T(8,128)(2,1)}), bf16[16,224,512]{2,1,0:T(8,128)(2,1)}, u32[]{:S(2)}, u32[]{:S(2)}) async-start(bf16[16,224,512]{2,1,0:T(8,128)(2,1)} %broadcast_select_fusion), calls=%async_computation.2 | async-start | bytes 7340032 | tf_op jit(solution)/shard_map/all_to_all | solution.py:66
  158.3 0.7 dynamic_slice.15
  161.1 0.1 copy.47
  161.2 0.3 copy.52
  161.5 0.3 copy.46
  161.7 65.5 %all-to-all-done.2 = bf16[16,224,512]{2,1,0:T(8,128)(2,1)} async-done(((bf16[16,224,512]{2,1,0:T(8,128)(2,1)}), bf16[16,224,512]{2,1,0:T(8,128)(2,1)}, u32[]{:S(2)}, u32[]{:S(2)}) %all-to-all-start.2) | async-done | bytes 3670048 | tf_op jit(solution)/shard_map/all_to_all | solution.py:66
  227.3 23.4 %while.21 = (s32[]{:T(128)}, bf16[8,16,512]{2,1,0:T(8,128)(2,1)S(1)}, bf16[8,16,3584]{2,1,0:T(8,128)(2,1)S(1)}, bf16[16,224,512]{2,1,0:T(8,128)(2,1)}, f32[28,4]{1,0:T(8,128)S(1)}, /*index=5*/s32[]{:T(128)}, f32[]{:T(128)}) while((s32[]{:T(128)}, bf16[8,16,512]{2,1,0:T(8,128)(2,1)S(1)}, bf16[8,16,3584]{2,1,0:T(8,128)(2,1)S(1)}, ...), condition=%wide.region_16.17_spmd, body=%wide.region_14.16_spmd.sunk | while | flops 59211776 | bytes 4694561 | solution.py:40
  227.3 0.1 broadcast_in_dim.88
  227.5 2.6 fusion.47
  230.2 0.1 broadcast_in_dim.88
  230.5 2.6 fusion.47
  233.2 0.1 broadcast_in_dim.88
  233.4 2.6 fusion.47
  236.1 0.1 broadcast_in_dim.88
  236.3 2.6 fusion.47
  239.0 0.1 broadcast_in_dim.88
  239.3 2.6 fusion.47
  242.0 0.1 broadcast_in_dim.88
  242.2 2.6 fusion.47
  244.9 0.1 broadcast_in_dim.88
  245.1 2.6 fusion.47
  247.8 0.1 broadcast_in_dim.88
  248.1 2.6 fusion.47
  250.7 0.7 copy.54
  251.5 17.2 %all-to-all-start.5 = ((bf16[8,16,512]{2,0,1:T(8,128)(2,1)}), bf16[8,16,512]{2,0,1:T(8,128)(2,1)S(1)}, u32[]{:S(2)}, u32[]{:S(2)}) async-start(bf16[8,16,512]{2,0,1:T(8,128)(2,1)} %copy.54), calls=%async_computation.5 | async-start | bytes 262144 | tf_op jit(solution)/shard_map/all_to_all | solution.py:41
  268.7 23.4 %while.20 = (s32[]{:T(128)}, bf16[8,16,512]{2,1,0:T(8,128)(2,1)S(1)}, bf16[8,16,3584]{2,1,0:T(8,128)(2,1)S(1)}, bf16[16,224,512]{2,1,0:T(8,128)(2,1)}, f32[28,4]{1,0:T(8,128)S(1)}, /*index=5*/s32[]{:T(128)}, f32[]{:T(128)}) while((s32[]{:T(128)}, bf16[8,16,512]{2,1,0:T(8,128)(2,1)S(1)}, bf16[8,16,3584]{2,1,0:T(8,128)(2,1)S(1)}, ...), condition=%wide.region_8.9_spmd, body=%wide.region_6.8_spmd.sunk | while | flops 59211776 | bytes 4694561 | solution.py:40
  268.7 0.1 broadcast_in_dim.87
  268.9 2.6 fusion.43
  271.6 0.1 broadcast_in_dim.87
  271.9 2.6 fusion.43
  274.8 2.6 fusion.43
  277.7 2.6 fusion.43
  280.6 2.6 fusion.43
  283.6 2.6 fusion.43
  286.5 2.6 fusion.43
  289.4 2.6 fusion.43
  292.1 0.7 copy.48
  292.8 6.0 %all-to-all-start.3 = ((bf16[8,16,512]{2,0,1:T(8,128)(2,1)}), bf16[8,16,512]{2,0,1:T(8,128)(2,1)S(1)}, u32[]{:S(2)}, u32[]{:S(2)}) async-start(bf16[8,16,512]{2,0,1:T(8,128)(2,1)} %copy.48), calls=%async_computation.3 | async-start | bytes 262144 | tf_op jit(solution)/shard_map/all_to_all | solution.py:41
  298.9 0.7 gather_fusion.2
  299.6 0.1 fusion.22
  299.7 6.0 %all-to-all-done.3 = bf16[8,16,512]{2,0,1:T(8,128)(2,1)S(1)} async-done(((bf16[8,16,512]{2,0,1:T(8,128)(2,1)}), bf16[8,16,512]{2,0,1:T(8,128)(2,1)S(1)}, u32[]{:S(2)}, u32[]{:S(2)}) %all-to-all-start.3) | async-done | bytes 131104 | tf_op jit(solution)/shard_map/all_to_all | solution.py:41
  305.8 0.7 gather_fusion.1
  306.5 0.1 fusion.23
  306.6 0.6 pad_maximum_fusion
  307.2 4.1 %copy.92 = bf16[1,3584,512]{2,1,0:T(8,128)(2,1)} copy(bf16[1,3584,512]{2,1,0:T(8,128)(2,1)} %bitcast.27) | data formatting | bytes 7340032
  (110 shorter events, 3.4 us)
Async XLA Ops:
  0.6 160.4 %copy-start = (f32[16,28,4]{1,2,0:T(4,128)S(1)}, f32[16,28,4]{1,2,0:T(4,128)}, u32[]{:S(2)}) copy-start(f32[16,28,4]{1,2,0:T(4,128)} %param.15) | copy-start | bytes 21508
  41.0 73.1 %all-to-all-start.1 = ((bf16[16,224,512]{2,1,0:T(8,128)(2,1)}), bf16[16,224,512]{2,1,0:T(8,128)(2,1)}, u32[]{:S(2)}, u32[]{:S(2)}) async-start(bf16[16,224,512]{2,1,0:T(8,128)(2,1)} %bitcast.113), calls=%async_computation.1 | async-start | bytes 7340032 | tf_op jit(solution)/shard_map/all_to_all | solution.py:68
  114.1 38.0 %all-to-all-start = ((bf16[8,16,3584]{2,0,1:T(8,128)(2,1)}), bf16[8,16,3584]{2,0,1:T(8,128)(2,1)S(1)}, u32[]{:S(2)}, u32[]{:S(2)}) async-start(bf16[8,16,3584]{2,0,1:T(8,128)(2,1)} %copy.45), calls=%async_computation | async-start | bytes 1835008 | tf_op jit(solution)/shard_map/all_to_all | solution.py:89
  140.3 18.0 %copy-start.2 = (s32[16]{0:T(128)S(1)}, s32[16]{0:T(128)}, u32[]{:S(2)}) copy-start(s32[16]{0:T(128)} %param.17) | copy-start | bytes 196
  140.3 20.9 %copy-start.1 = (f32[2,8,8]{2,1,0:T(8,128)S(1)}, f32[2,8,8]{2,1,0:T(8,128)}, u32[]{:S(2)}) copy-start(f32[2,8,8]{2,1,0:T(8,128)} %param.13) | copy-start | bytes 1540
  152.2 75.1 %all-to-all-start.2 = ((bf16[16,224,512]{2,1,0:T(8,128)(2,1)}), bf16[16,224,512]{2,1,0:T(8,128)(2,1)}, u32[]{:S(2)}, u32[]{:S(2)}) async-start(bf16[16,224,512]{2,1,0:T(8,128)(2,1)} %broadcast_select_fusion), calls=%async_computation.2 | async-start | bytes 7340032 | tf_op jit(solution)/shard_map/all_to_all | solution.py:66
  251.5 41.4 %all-to-all-start.5 = ((bf16[8,16,512]{2,0,1:T(8,128)(2,1)}), bf16[8,16,512]{2,0,1:T(8,128)(2,1)S(1)}, u32[]{:S(2)}, u32[]{:S(2)}) async-start(bf16[8,16,512]{2,0,1:T(8,128)(2,1)} %copy.54), calls=%async_computation.5 | async-start | bytes 262144 | tf_op jit(solution)/shard_map/all_to_all | solution.py:41
  292.8 12.9 %all-to-all-start.3 = ((bf16[8,16,512]{2,0,1:T(8,128)(2,1)}), bf16[8,16,512]{2,0,1:T(8,128)(2,1)S(1)}, u32[]{:S(2)}, u32[]{:S(2)}) async-start(bf16[8,16,512]{2,0,1:T(8,128)(2,1)} %copy.48), calls=%async_computation.3 | async-start | bytes 262144 | tf_op jit(solution)/shard_map/all_to_all | solution.py:41
where the time goes:
time: 314 us; the launch traced here: 311 us
  waiting for transfers between devices  149 us (47%)
  starting transfers between devices  51 us (16%)
  matrix products  42.2 us (13%)
  blocking collectives  34.9 us (11%)
  local copies, waits for them, and re-layouts  23.2 us (7%)
  other arithmetic  7.1 us (2%)
    all_to_all x1, waiting for transfers between devices, shards(): lax.all_to_all(pieces, 'ep', split_axis=0, concat_axis=0, tiled=True)  65.7 us
    all_to_all x1, waiting for transfers between devices, shards(): lax.all_to_all(jnp.take(lax.all_to_all(pieces, 'ep', split_axis=0, concat...  65.5 us
    dot_general x16, matrix products, scaled_product(): jnp.einsum('rbi,bif->rbf', token_rows.reshape(token_rows.shape[0], row_bl...  42.2 us
    all_to_all x1, blocking collectives, shards(): lax.all_to_all(send_buffer, 'ep', split_axis=1, concat_axis=1, tiled=True)  30.7 us
    all_to_all x2, starting transfers between devices, serve_rows(): lax.all_to_all(activated, 'ep', split_axis=1, concat_axis=1, tiled=True)  23.2 us
    all_to_all x1, starting transfers between devices, shards(): lax.all_to_all(send_buffer, 'ep', split_axis=1, concat_axis=1, tiled=True)  17.2 us
    all_to_all x1, waiting for transfers between devices, shards(): lax.all_to_all(send_buffer, 'ep', split_axis=1, concat_axis=1, tiled=True)  11.8 us
  transfers between devices with their start and end apart: 5, of which 4 were waited for; matrix products, arithmetic and copies ran while one was open for 12% of the time, Pallas kernels for 0%

commit v1 on v0

v1 whole, which is shorter than its diff:
```python
import functools

import jax
import jax.numpy as jnp
import numpy as np
from jax import lax
from jax.experimental import pallas as pl
from jax.experimental.pallas import tpu as pltpu
from jax.sharding import PartitionSpec as P

MESH = pl.DeviceIdType.MESH
MOVED_BITS = 4
CHUNKS = 2


def inverse_place(expert_at):
    count = expert_at.shape[0]
    labels = jnp.arange(count, dtype=jnp.int32)
    match = expert_at[None, :] == labels[:, None]
    return jnp.sum(jnp.where(match, labels[None, :], 0), axis=1)


def source_slots(old_expert, new_expert):
    labels = jnp.arange(old_expert.shape[0], dtype=jnp.int32)
    match = old_expert[None, :] == new_expert[:, None]
    return jnp.sum(jnp.where(match, labels[None, :], 0), axis=1)


def parity(number):
    return bin(number).count("1") % 2


def halves():
    return [(mask, side) for mask in range(1, 16) for side in range(2)]


def half_members(mask, side):
    return [s for s in range(16) if parity(s & mask) == side]


def free_bits(mask):
    pivot = min(j for j in range(MOVED_BITS) if mask >> j & 1)
    return [j for j in range(MOVED_BITS) if j != pivot]


def rank_in_half(mask, slot):
    return sum((slot >> j & 1) << i for i, j in enumerate(free_bits(mask)))


def relocate_kernel(mask, side, ranks_ref, x_ref, o_ref, *scratch):
    got, stage = scratch[:CHUNKS], scratch[CHUNKS : 2 * CHUNKS]
    send_sem, recv_sem, own_sem = scratch[2 * CHUNKS :]
    me = lax.axis_index("ep")
    bits = [lax.rem(me // (1 << j), 2) for j in range(MOVED_BITS)]
    flips = [1 - 2 * bit for bit in bits]
    my_parity = lax.rem(sum(bits[j] for j in range(MOVED_BITS) if mask >> j & 1), 2)
    kept = free_bits(mask)
    rank = sum(bits[j] * (1 << i) for i, j in enumerate(kept))
    turns = [t for t in range(1, 16) if parity(t & mask) == 0]

    def partner(turn):
        slot = me + sum(flips[j] * (1 << j) for j in range(MOVED_BITS) if turn >> j & 1)
        its_rank = rank + sum(flips[j] * (1 << i) for i, j in enumerate(kept) if turn >> j & 1)
        return slot, its_rank

    @pl.when(my_parity != side)
    def _():
        copy = pltpu.make_async_copy(x_ref, o_ref, own_sem.at[0, 0])
        copy.start()
        copy.wait()

    @pl.when(my_parity == side)
    def _():
        def scatter(chunk, i, turn):
            slot, its_rank = partner(turn)
            return pltpu.make_async_remote_copy(
                src_ref=x_ref.at[its_rank, chunk],
                dst_ref=got[chunk].at[rank],
                send_sem=send_sem.at[0, chunk, i],
                recv_sem=recv_sem.at[0, chunk, i],
                device_id={"ep": slot},
                device_id_type=MESH,
            )

        def gather(chunk, i, turn):
            slot, its_rank = partner(turn)
            return pltpu.make_async_remote_copy(
                src_ref=stage[chunk].at[its_rank],
                dst_ref=o_ref.at[rank, chunk],
                send_sem=send_sem.at[1, chunk, i],
                recv_sem=recv_sem.at[1, chunk, i],
                device_id={"ep": slot},
                device_id_type=MESH,
            )

        def own_in(chunk):
            return pltpu.make_async_copy(x_ref.at[rank, chunk], got[chunk].at[rank], own_sem.at[0, chunk])

        def own_out(chunk):
            return pltpu.make_async_copy(stage[chunk].at[rank], o_ref.at[rank, chunk], own_sem.at[1, chunk])

        for chunk in range(CHUNKS):
            for i, turn in enumerate(turns):
                scatter(chunk, i, turn).start()
            own_in(chunk).start()
        for chunk in range(CHUNKS):
            own_in(chunk).wait()
            for i, turn in enumerate(turns):
                scatter(chunk, i, turn).wait_recv()

            def place(index, carry, chunk=chunk):
                stage[chunk][index] = got[chunk][ranks_ref[index]]
                return carry

            lax.fori_loop(0, 8, place, 0)
            for i, turn in enumerate(turns):
                gather(chunk, i, turn).start()
            own_out(chunk).start()
        for chunk in range(CHUNKS):
            own_out(chunk).wait()
            for i, turn in enumerate(turns):
                scatter(chunk, i, turn).wait_send()
                gather(chunk, i, turn).wait()


def relocate(old_block, old_expert, new_expert):
    depth, width = old_block.shape
    rows = depth // (8 * CHUNKS)
    sources = source_slots(old_expert, new_expert)
    moved = (old_expert != new_expert).astype(jnp.int32)
    table = np.array([[parity(s & mask) == side for s in range(16)] for mask, side in halves()], np.int32)
    chosen = jnp.argmax(jnp.sum(jnp.asarray(table) * moved[None, :], axis=1)).astype(jnp.int32)

    def branch(mask, side):
        members = np.array(half_members(mask, side), np.int32)
        members = members[np.argsort([rank_in_half(mask, s) for s in members])]
        rank_of = np.array([rank_in_half(mask, s) for s in range(16)], np.int32)

        def run(block, sources):
            ranks = jnp.asarray(rank_of)[sources[members]]
            piece = (8, rows, width)
            return pl.pallas_call(
                functools.partial(relocate_kernel, mask, side),
                out_shape=jax.ShapeDtypeStruct((8, CHUNKS, rows, width), block.dtype),
                in_specs=[pl.BlockSpec(memory_space=pltpu.SMEM), pl.BlockSpec(memory_space=pl.ANY)],
                out_specs=pl.BlockSpec(memory_space=pl.ANY),
                scratch_shapes=[pltpu.VMEM(piece, block.dtype)] * (2 * CHUNKS)
                + [
                    pltpu.SemaphoreType.DMA((2, CHUNKS, 7)),
                    pltpu.SemaphoreType.DMA((2, CHUNKS, 7)),
                    pltpu.SemaphoreType.DMA((2, CHUNKS)),
                ],
                compiler_params=pltpu.CompilerParams(has_side_effects=True, vmem_limit_bytes=32 << 20),
                name=f"relocate_{mask}_{side}",
            )(ranks, block)

        return run

    pieces = old_block.reshape(8, CHUNKS, rows, width)
    moved_pieces = lax.switch(chosen, [branch(*half) for half in halves()], pieces, sources)
    return moved_pieces.reshape(depth, width)


def serve_kernel(steps, block_rows, blocks, x_ref, w_ref, s_ref, o_ref, total):
    step = pl.program_id(0)

    @pl.when(step == 0)
    def _():
        total[...] = jnp.zeros_like(total)

    value = total[...]
    for i in range(blocks):
        rows = pl.ds(i * block_rows, block_rows)
        product = jnp.dot(x_ref[:, rows], w_ref[rows, :], preferred_element_type=jnp.float32)
        value = value + product * s_ref[0, i : i + 1, :]
    total[...] = value

    @pl.when(step == steps - 1)
    def _():
        u = total[...]
        o_ref[...] = (u / (1.0 + jnp.exp(-u))).astype(o_ref.dtype)


def serve(rows, block, scales):
    count, depth = rows.shape
    width = block.shape[1]
    row_blocks = scales.shape[0]
    block_rows = depth // row_blocks
    blocks = 4
    steps = row_blocks // blocks
    widened = jnp.repeat(scales, width // scales.shape[1], axis=1).reshape(steps, blocks, width)
    return pl.pallas_call(
        functools.partial(serve_kernel, steps, block_rows, blocks),
        out_shape=jax.ShapeDtypeStruct((count, width), jnp.bfloat16),
        grid=(steps,),
        in_specs=[
            pl.BlockSpec((count, blocks * block_rows), lambda i: (0, i)),
            pl.BlockSpec((blocks * block_rows, width), lambda i: (i, 0)),
            pl.BlockSpec((1, blocks, width), lambda i: (i, 0, 0)),
        ],
        out_specs=pl.BlockSpec((count, width), lambda i: (0, 0)),
        scratch_shapes=[pltpu.VMEM((count, width), jnp.float32)],
        compiler_params=pltpu.CompilerParams(vmem_limit_bytes=32 << 20),
        cost_estimate=pl.CostEstimate(
            flops=2 * count * depth * width, bytes_accessed=2 * depth * (count + width), transcendentals=count * width
        ),
        name="serve",
    )(rows, block, widened)


def relocate_any(old_block, old_expert, new_expert):
    peers = lax.axis_size("ep")
    sources = source_slots(old_expert, new_expert)
    pieces = old_block.reshape(peers, old_block.shape[0] // peers, old_block.shape[1])
    gathered = lax.all_to_all(pieces, "ep", split_axis=0, concat_axis=0, tiled=True)
    placed = lax.map(lambda s: lax.dynamic_index_in_dim(gathered, s, keepdims=False), sources)
    return lax.all_to_all(placed, "ep", split_axis=0, concat_axis=0, tiled=True).reshape(old_block.shape)


def served(tokens, routing, gate_values, old_block, scales, old_expert):
    peers = lax.axis_size("ep")
    steps, group, _ = routing.shape
    depth, width = old_block.shape
    everyone = lax.all_gather(tokens, ("ep", "dp"), axis=1, tiled=True)
    act = serve(everyone.reshape(-1, depth), old_block, scales).reshape(steps, peers, group, width)
    returned = lax.all_to_all(act, "ep", split_axis=1, concat_axis=1, tiled=True)
    gates = jnp.sum(
        jnp.where(old_expert[None, None, None, :] == routing[..., None], gate_values[..., None], 0.0), axis=2
    )
    weighted = jnp.sum(jnp.transpose(gates, (0, 2, 1))[..., None] * returned.astype(jnp.float32), axis=1)
    return weighted.astype(jnp.bfloat16)


def shards(tokens, routing, gate_values, held_weight, scale_table, old_expert, new_expert):
    old_block = held_weight[0]
    scales = scale_table[old_expert[lax.axis_index("ep")]]
    if lax.axis_size("ep") == 16:
        combined = served(tokens, routing, gate_values, old_block, scales, old_expert)
        new_block = relocate(old_block, old_expert, new_expert)
    else:
        done = []
        for n in range(tokens.shape[0]):
            step = (tokens[n : n + 1], routing[n : n + 1], gate_values[n : n + 1])
            if done:
                step, done[-1] = lax.optimization_barrier((step, done[-1]))
            done.append(served(*step, old_block, scales, old_expert))
        combined = jnp.concatenate(done)
        new_block = relocate_any(old_block, old_expert, new_expert)
    return combined, new_block[None]


def solution(mesh):
    placed = (
        P(None, ("ep", "dp"), None),
        P(None, "ep", None),
        P(None, "ep", None),
        P("ep", None, "dp"),
        P(None, None, "dp"),
        P(),
        P(),
    )
    return jax.shard_map(
        shards,
        mesh=mesh,
        in_specs=placed,
        out_specs=(P(None, "ep", "dp"), P("ep", None, "dp")),
        check_vma=False,
    )
```

time: 314 us -> 217 us (0.69); the launches traced: 311 us -> 219 us
  Pallas kernels: 0 us -> 122 us
  waiting for transfers between devices: 149 us -> 55.9 us
  starting transfers between devices: 51 us -> 4.72 us
  matrix products: 42.2 us -> 0 us
  blocking collectives: 34.9 us -> 0 us
  between operations: 2.87 us -> 16.7 us
  local copies, waits for them, and re-layouts: 23.2 us -> 11.7 us
  loops' own time: 0.99 us -> 4.69 us
  other arithmetic: 7.1 us -> 3.85 us
    all_to_all x5 -> x1, waiting for transfers between devices: 149 us -> 0.01 us  [served(): lax.all_to_all(act, 'ep', split_axis=1, concat_axis=1, tiled=True)]
    pallas_call x0 -> x2, Pallas kernels: none -> 122 us  [the longest x1 118 us: run(): pl.pallas_call(functools.partial(relocate_kernel, mask, side), out_shape=...]
    all_gather x0 -> x1, waiting for transfers between devices: none -> 55.8 us  [served(): everyone = lax.all_gather(tokens, ('ep', 'dp'), axis=1, tiled=True)]
    all_to_all x5 -> x1, starting transfers between devices: 51 us -> 4.69 us  [served(): lax.all_to_all(act, 'ep', split_axis=1, concat_axis=1, tiled=True)]
    dot_general x16 -> x0, matrix products: 42.2 us -> none  [scaled_product(): jnp.einsum('rbi,bif->rbf', token_rows.reshape(token_rows.shape[0], row_bl...]
    all_to_all x1 -> x0, blocking collectives: 30.7 us -> none  [shards(): lax.all_to_all(send_buffer, 'ep', split_axis=1, concat_axis=1, tiled=True)]
    gather x3 -> x2, local copies, waits for them, and re-layouts: 6.06 us -> 1.29 us  [run(): ranks = jnp.asarray(rank_of)[sources[members]]]
    all_gather x1 -> x0, blocking collectives: 4.26 us -> none  [shards(): grouped = lax.all_gather(tokens, 'dp', axis=1, tiled=True)]
  transfers between devices with their start and end apart: 5 -> 2, of which waited for: 4 -> 1; matrix products, arithmetic and copies ran while one was open for 12% -> 3% of each run, Pallas kernels for 0% -> 54%
where the time goes in v1:
time: 217 us; the launch traced here: 219 us
  Pallas kernels  122 us (56%)
  waiting for transfers between devices  55.9 us (26%)
  between operations  16.7 us (8%)
  local copies, waits for them, and re-layouts  11.7 us (5%)
  starting transfers between devices  4.72 us (2%)
  loops' own time  4.69 us (2%)
  other arithmetic  3.85 us (2%)
    pallas_call x1, Pallas kernels, run(): pl.pallas_call(functools.partial(relocate_kernel, mask, side), out_shape=...  118 us
    all_gather x1, waiting for transfers between devices, served(): everyone = lax.all_gather(tokens, ('ep', 'dp'), axis=1, tiled=True)  55.8 us
    unnamed x16, local copies, waits for them, and re-layouts  6.33 us
    another operation x1, loops' own time, relocate(): lax.switch(chosen, [branch(*half) for half in halves()], pieces, sources)  4.69 us
    all_to_all x1, starting transfers between devices, served(): lax.all_to_all(act, 'ep', split_axis=1, concat_axis=1, tiled=True)  4.69 us
  transfers between devices with their start and end apart: 2, of which 1 were waited for; matrix products, arithmetic and copies ran while one was open for 3% of the time, Pallas kernels for 54%

profile of v1, /device:TPU:1, one launch (start us, length us, event | category | flops | bytes accessed | tf_op | source)
XLA Modules:
  0.0 219.2 jit_solution(12904409680971032295)
XLA Ops:
  7.2 0.0 copy-start
  7.2 0.0 all-gather.2.cloned.1.call-start
  7.2 1.5 copy.166
  8.7 0.0 all-gather.2.cloned.1.call-update
  8.7 1.2 dynamic_slice.6
  11.3 0.9 select_reduce_fusion.1
  12.2 0.8 select_reduce_fusion
  13.0 0.1 copy.165
  13.7 0.0 copy-done
  13.8 0.1 copy.168
  13.9 0.1 broadcast_in_dim.157
  14.0 55.8 %all-gather.2.cloned.1.call-done = bf16[2,128,3584]{2,0,1:T(2,128)(2,1)} async-done(((bf16[2,4,3584]{2,0,1:T(2,128)(2,1)}), bf16[2,128,3584]{2,0,1:T(2,128)(2,1)}) %all-gather.2.cloned.1.call-update) | async-done | bytes 1835024 | tf_op jit(solution)/shard_map/all_gather | solution.py:224
  69.8 0.0 copy-start.2
  69.8 1.8 copy.167
  71.7 0.0 copy-start.5
  71.7 0.0 copy-start.6
  71.7 0.0 copy-start.4
  71.7 0.0 copy-start.1
  71.7 0.0 copy-start.3
  71.7 0.7 copy-done.2
  72.4 3.4 %serve.1 = bf16[256,512]{1,0:T(8,128)(2,1)S(1)} custom-call(bf16[256,3584]{1,0:T(8,128)(2,1)S(1)} %bitcast.194, bf16[3584,512]{1,0:T(8,128)(2,1)S(1)} %bitcast.226, f32[7,4,512]{2,1,0:T(4,128)S(1)} %reshape_reshape.3.s_ref), custom_call_target="tpu_custom_call" | custom-call | flops 939524096 | bytes 5505024 | tf_op jit(solution)/shard_map/serve/pallas_call | solution.py:192
  75.8 0.7 copy.169
  76.5 4.7 %all-to-all-start = ((bf16[2,16,8,512]{3,2,0,1:T(8,128)(2,1)}), bf16[2,16,8,512]{3,2,0,1:T(8,128)(2,1)S(1)}, u32[]{:S(2)}, u32[]{:S(2)}) async-start(bf16[2,16,8,512]{3,2,0,1:T(8,128)(2,1)} %copy.169), calls=%async_computation | async-start | bytes 524288 | tf_op jit(solution)/shard_map/all_to_all | solution.py:226
  81.2 0.0 copy-done.5
  81.2 0.0 copy-done.6
  81.3 0.0 copy-done.4
  81.3 0.1 multiply_reduce_fusion.1
  81.4 0.7 iota_reduce_fusion
  82.0 0.0 copy-done.1
  82.0 0.0 copy-done.3
  82.6 124.9 %conditional.1 = (bf16[1,3584,512]{2,1,0:T(8,128)(2,1)}) conditional(s32[]{:T(128)} %clamp.3, (s32[8]{0:T(128)S(1)}, pred[8]{0:T(512)(128)(4,1)S(1)}, s32[16]{0:T(128)S(1)}, s32[16]{0:T(128)S(1)}, bf16[8,2,224,512]{3,2,1,0:T(8,128)(2,1)}) %tuple.296, (pred[8]{0:T(512)(128)(4,1)S(1)}, s32[16]{0:T(128)S(1)}, ...), branch_computations={%region_5.6_spmd.clone, %region_6.7_spmd.clone, %region_7.8_spmd.c... | conditional | flops 2096 | bytes 8624 | solution.py:160
  82.6 0.7 select_n.442
  83.3 0.6 gather_fusion.20
  84.0 0.6 gather_fusion.21
  84.6 118.2 %relocate_9_0.1 = bf16[8,2,224,512]{3,2,1,0:T(8,128)(2,1)} custom-call(s32[8]{0:T(128)S(1)} %gather_fusion.21, bf16[8,2,224,512]{3,2,1,0:T(8,128)(2,1)} %get-tuple-element.674.x_ref), custom_call_target="tpu_custom_call" | custom-call | tf_op jit(solution)/shard_map/cond/branch_16_fun/relocate_9_0/pallas_call | solution.py:142
  207.5 0.0 all-to-all-done
  207.5 0.7 multiply_reduce_fusion
  208.2 4.1 %copy.201 = bf16[1,3584,512]{2,1,0:T(8,128)(2,1)} copy(bf16[1,3584,512]{2,1,0:T(8,128)(2,1)} %get-tuple-element.859) | data formatting | bytes 7340032
  (9 shorter events, 0.1 us)
Async XLA Ops:
  7.2 6.6 %copy-start = (f32[16,28,4]{1,2,0:T(4,128)S(1)}, f32[16,28,4]{1,2,0:T(4,128)}, u32[]{:S(2)}) copy-start(f32[16,28,4]{1,2,0:T(4,128)} %param.132) | copy-start | bytes 21508
  7.2 62.7 %all-gather.2.cloned.1.call-start = ((), (), s32[]{:S(2)}) async-start(), calls=%async_computation.1 | async-start | bytes 1892352 | tf_op jit(solution)/shard_map/all_gather | solution.py:224
  69.8 2.6 %copy-start.2 = (bf16[1,3584,512]{2,1,0:T(8,128)(2,1)S(1)}, bf16[1,3584,512]{2,1,0:T(8,128)(2,1)}, u32[]{:S(2)}) copy-start(bf16[1,3584,512]{2,1,0:T(8,128)(2,1)} %param.131) | copy-start | bytes 11010052
  71.7 9.6 %copy-start.5 = (s32[16]{0:T(128)S(1)}, s32[16]{0:T(128)}, u32[]{:S(2)}) copy-start(s32[16]{0:T(128)} %param.133) | copy-start | bytes 196
  71.7 9.6 %copy-start.6 = (s32[16]{0:T(128)S(1)}, s32[16]{0:T(128)}, u32[]{:S(2)}) copy-start(s32[16]{0:T(128)} %param.134) | copy-start | bytes 196
  71.7 9.6 %copy-start.4 = (s32[30,16]{0,1:T(8,128)S(1)}, s32[30,16]{0,1:T(8,128)}, u32[]{:S(2)}) copy-start(s32[30,16]{0,1:T(8,128)} %constant.212.clone) | copy-start | bytes 5764
  71.7 10.3 %copy-start.1 = (s32[16]{0:T(128)S(1)}, s32[16]{0:T(128)}, u32[]{:S(2)}) copy-start(s32[16]{0:T(128)} %constant.213.clone) | copy-start | bytes 196
  71.7 10.3 %copy-start.3 = (s32[16]{0:T(128)S(1)}, s32[16]{0:T(128)}, u32[]{:S(2)}) copy-start(s32[16]{0:T(128)} %constant.231.clone) | copy-start | bytes 196
  76.5 130.9 %all-to-all-start = ((bf16[2,16,8,512]{3,2,0,1:T(8,128)(2,1)}), bf16[2,16,8,512]{3,2,0,1:T(8,128)(2,1)S(1)}, u32[]{:S(2)}, u32[]{:S(2)}) async-start(bf16[2,16,8,512]{3,2,0,1:T(8,128)(2,1)} %copy.169), calls=%async_computation | async-start | bytes 524288 | tf_op jit(solution)/shard_map/all_to_all | solution.py:226
Sparse Core Ops, SparseCore 0:
  11.5 58.3 all-gather.1

commit v2 on v1

--- a/solution.py
+++ b/solution.py
@@ -31,11 +31,8 @@
 
 
 def halves():
-    return [(mask, side) for mask in range(1, 16) for side in range(2)]
-
-
-def half_members(mask, side):
-    return [s for s in range(16) if parity(s & mask) == side]
+    masks = sorted(range(1, 16), key=lambda mask: (mask in (2, 10), mask))
+    return [(mask, side) for mask in masks for side in range(2)]
 
 
 def free_bits(mask):
@@ -43,11 +40,7 @@
     return [j for j in range(MOVED_BITS) if j != pivot]
 
 
-def rank_in_half(mask, slot):
-    return sum((slot >> j & 1) << i for i, j in enumerate(free_bits(mask)))
-
-
-def relocate_kernel(mask, side, ranks_ref, x_ref, o_ref, *scratch):
+def relocate_kernel(mask, side, sources_ref, x_ref, o_ref, *scratch):
     got, stage = scratch[:CHUNKS], scratch[CHUNKS : 2 * CHUNKS]
     send_sem, recv_sem, own_sem = scratch[2 * CHUNKS :]
     me = lax.axis_index("ep")
@@ -63,11 +56,28 @@
         its_rank = rank + sum(flips[j] * (1 << i) for i, j in enumerate(kept) if turn >> j & 1)
         return slot, its_rank
 
+    def source_rank(index):
+        pivot = min(j for j in range(MOVED_BITS) if mask >> j & 1)
+        digits = {j: lax.rem(index // (1 << i), 2) for i, j in enumerate(kept)}
+        digits[pivot] = lax.rem(side + sum(digits[j] for j in kept if mask >> j & 1), 2)
+        source = sources_ref[sum(digits[j] * (1 << j) for j in range(MOVED_BITS))]
+        return sum(lax.rem(source // (1 << j), 2) * (1 << i) for i, j in enumerate(kept))
+
     @pl.when(my_parity != side)
     def _():
-        copy = pltpu.make_async_copy(x_ref, o_ref, own_sem.at[0, 0])
-        copy.start()
-        copy.wait()
+        def pass_in(chunk):
+            return pltpu.make_async_copy(x_ref.at[:, chunk], got[chunk], own_sem.at[0, chunk])
+
+        def pass_out(chunk):
+            return pltpu.make_async_copy(got[chunk], o_ref.at[:, chunk], own_sem.at[1, chunk])
+
+        for chunk in range(CHUNKS):
+            pass_in(chunk).start()
+        for chunk in range(CHUNKS):
+            pass_in(chunk).wait()
+            pass_out(chunk).start()
+        for chunk in range(CHUNKS):
+            pass_out(chunk).wait()
 
     @pl.when(my_parity == side)
     def _():
@@ -109,7 +119,7 @@
                 scatter(chunk, i, turn).wait_recv()
 
             def place(index, carry, chunk=chunk):
-                stage[chunk][index] = got[chunk][ranks_ref[index]]
+                stage[chunk][index] = got[chunk][source_rank(index)]
                 return carry
 
             lax.fori_loop(0, 8, place, 0)
@@ -132,12 +142,7 @@
     chosen = jnp.argmax(jnp.sum(jnp.asarray(table) * moved[None, :], axis=1)).astype(jnp.int32)
 
     def branch(mask, side):
-        members = np.array(half_members(mask, side), np.int32)
-        members = members[np.argsort([rank_in_half(mask, s) for s in members])]
-        rank_of = np.array([rank_in_half(mask, s) for s in range(16)], np.int32)
-
         def run(block, sources):
-            ranks = jnp.asarray(rank_of)[sources[members]]
             piece = (8, rows, width)
             return pl.pallas_call(
                 functools.partial(relocate_kernel, mask, side),
@@ -152,7 +157,7 @@
                 ],
                 compiler_params=pltpu.CompilerParams(has_side_effects=True, vmem_limit_bytes=32 << 20),
                 name=f"relocate_{mask}_{side}",
-            )(ranks, block)
+            )(sources, block)
 
         return run
 
@@ -161,8 +166,12 @@
     return moved_pieces.reshape(depth, width)
 
 
-def serve_kernel(steps, block_rows, blocks, x_ref, w_ref, s_ref, o_ref, total):
+def serve_kernel(steps, block_rows, blocks, x_ref, w_ref, s_ref, *rest):
+    *passed, total = rest
+    o_ref = passed[-1]
     step = pl.program_id(0)
+    if len(passed) == 3:
+        passed[1][...] = passed[0][...]
 
     @pl.when(step == 0)
     def _():
@@ -181,7 +190,7 @@
         o_ref[...] = (u / (1.0 + jnp.exp(-u))).astype(o_ref.dtype)
 
 
-def serve(rows, block, scales):
+def serve(rows, block, scales, moved=None):
     count, depth = rows.shape
     width = block.shape[1]
     row_blocks = scales.shape[0]
@@ -189,23 +198,30 @@
     blocks = 4
     steps = row_blocks // blocks
     widened = jnp.repeat(scales, width // scales.shape[1], axis=1).reshape(steps, blocks, width)
+    weights = pl.BlockSpec((blocks * block_rows, width), lambda i: (i, 0))
+    act = jax.ShapeDtypeStruct((count, width), jnp.bfloat16)
+    act_spec = pl.BlockSpec((count, width), lambda i: (0, 0))
+    extra = [] if moved is None else [moved]
     return pl.pallas_call(
         functools.partial(serve_kernel, steps, block_rows, blocks),
-        out_shape=jax.ShapeDtypeStruct((count, width), jnp.bfloat16),
+        out_shape=[jax.ShapeDtypeStruct(e.shape, e.dtype) for e in extra] + [act],
         grid=(steps,),
         in_specs=[
             pl.BlockSpec((count, blocks * block_rows), lambda i: (0, i)),
-            pl.BlockSpec((blocks * block_rows, width), lambda i: (i, 0)),
+            weights,
             pl.BlockSpec((1, blocks, width), lambda i: (i, 0, 0)),
-        ],
-        out_specs=pl.BlockSpec((count, width), lambda i: (0, 0)),
+        ]
+        + [weights] * len(extra),
+        out_specs=[weights] * len(extra) + [act_spec],
         scratch_shapes=[pltpu.VMEM((count, width), jnp.float32)],
         compiler_params=pltpu.CompilerParams(vmem_limit_bytes=32 << 20),
         cost_estimate=pl.CostEstimate(
-            flops=2 * count * depth * width, bytes_accessed=2 * depth * (count + width), transcendentals=count * width
+            flops=2 * count * depth * width,
+            bytes_accessed=2 * depth * (count + (1 + 2 * len(extra)) * width),
+            transcendentals=count * width,
         ),
         name="serve",
-    )(rows, block, widened)
+    )(rows, block, widened, *extra)
 
 
 def relocate_any(old_block, old_expert, new_expert):
@@ -217,33 +233,39 @@
     return lax.all_to_all(placed, "ep", split_axis=0, concat_axis=0, tiled=True).reshape(old_block.shape)
 
 
-def served(tokens, routing, gate_values, old_block, scales, old_expert):
+def served(tokens, routing, gate_values, old_block, scales, old_expert, moved=None):
     peers = lax.axis_size("ep")
     steps, group, _ = routing.shape
     depth, width = old_block.shape
-    everyone = lax.all_gather(tokens, ("ep", "dp"), axis=1, tiled=True)
-    act = serve(everyone.reshape(-1, depth), old_block, scales).reshape(steps, peers, group, width)
-    returned = lax.all_to_all(act, "ep", split_axis=1, concat_axis=1, tiled=True)
+    mine = jnp.transpose(tokens, (1, 0, 2)).reshape(-1, depth)
+    everyone = lax.all_gather(mine, ("ep", "dp"), axis=0, tiled=True)
+    *passed, act = serve(everyone, old_block, scales, moved)
+    act = act.reshape(peers, group * steps, width)
+    returned = lax.all_to_all(act, "ep", split_axis=0, concat_axis=0, tiled=True)
     gates = jnp.sum(
-        jnp.where(old_expert[None, None, None, :] == routing[..., None], gate_values[..., None], 0.0), axis=2
+        jnp.where(old_expert[:, None, None, None] == routing[None], gate_values[None], 0.0), axis=3
     )
-    weighted = jnp.sum(jnp.transpose(gates, (0, 2, 1))[..., None] * returned.astype(jnp.float32), axis=1)
-    return weighted.astype(jnp.bfloat16)
+    gates = jnp.transpose(gates, (0, 2, 1)).reshape(peers, group * steps)
+    weighted = jnp.sum(gates[:, :, None] * returned.astype(jnp.float32), axis=0)
+    weighted = weighted.astype(jnp.bfloat16).reshape(group, steps, width)
+    return jnp.transpose(weighted, (1, 0, 2)), *passed
 
 
 def shards(tokens, routing, gate_values, held_weight, scale_table, old_expert, new_expert):
     old_block = held_weight[0]
     scales = scale_table[old_expert[lax.axis_index("ep")]]
     if lax.axis_size("ep") == 16:
-        combined = served(tokens, routing, gate_values, old_block, scales, old_expert)
         new_block = relocate(old_block, old_expert, new_expert)
+        combined, new_block = served(
+            tokens, routing, gate_values, old_block, scales, old_expert, new_block
+        )
     else:
         done = []
         for n in range(tokens.shape[0]):
             step = (tokens[n : n + 1], routing[n : n + 1], gate_values[n : n + 1])
             if done:
                 step, done[-1] = lax.optimization_barrier((step, done[-1]))
-            done.append(served(*step, old_block, scales, old_expert))
+            done += served(*step, old_block, scales, old_expert)
         combined = jnp.concatenate(done)
         new_block = relocate_any(old_block, old_expert, new_expert)
     return combined, new_block[None]

time: 217 us -> 148 us (0.68); the launches traced: 219 us -> 147 us
  waiting for transfers between devices: 55.9 us -> 9.3 us
  Pallas kernels: 122 us -> 105 us
  local copies, waits for them, and re-layouts: 11.7 us -> 5.2 us
  loops' own time: 4.69 us -> 0.29 us
  starting transfers between devices: 4.72 us -> 6.91 us
    all_gather x1, waiting for transfers between devices: 55.8 us -> 0.02 us  [served(): everyone = lax.all_gather(mine, ('ep', 'dp'), axis=0, tiled=True)]
    pallas_call x1, Pallas kernels: 118 us -> 96.6 us  [run(): pl.pallas_call(functools.partial(relocate_kernel, mask, side), out_shape=...]
    all_to_all x1, waiting for transfers between devices: 0.01 us -> 9.27 us  [served(): lax.all_to_all(act, 'ep', split_axis=0, concat_axis=0, tiled=True)]
    pallas_call x1, Pallas kernels: 3.38 us -> 8.42 us  [serve(): pl.pallas_call(functools.partial(serve_kernel, steps, block_rows, blocks)...]
    another operation x1, loops' own time: 4.69 us -> 0.29 us  [relocate(): lax.switch(chosen, [branch(*half) for half in halves()], pieces, sources)]
    unnamed x16 -> x11, local copies, waits for them, and re-layouts: 6.33 us -> 2.12 us
    all_to_all x1, starting transfers between devices: 4.69 us -> 6.87 us  [served(): lax.all_to_all(act, 'ep', split_axis=0, concat_axis=0, tiled=True)]
  transfers between devices with their start and end apart: 2 -> 2, of which waited for: 1 -> 1; matrix products, arithmetic and copies ran while one was open for 3% -> 3% of each run, Pallas kernels for 54% -> 66%
where the time goes in v2:
time: 148 us; the launch traced here: 147 us
  Pallas kernels  105 us (71%)
  between operations  16.8 us (11%)
  waiting for transfers between devices  9.3 us (6%)
  starting transfers between devices  6.91 us (5%)
  local copies, waits for them, and re-layouts  5.2 us (4%)
  other arithmetic  3.27 us (2%)
    pallas_call x1, Pallas kernels, run(): pl.pallas_call(functools.partial(relocate_kernel, mask, side), out_shape=...  96.6 us
    all_to_all x1, waiting for transfers between devices, served(): lax.all_to_all(act, 'ep', split_axis=0, concat_axis=0, tiled=True)  9.27 us
    pallas_call x1, Pallas kernels, serve(): pl.pallas_call(functools.partial(serve_kernel, steps, block_rows, blocks)...  8.42 us
    all_to_all x1, starting transfers between devices, served(): lax.all_to_all(act, 'ep', split_axis=0, concat_axis=0, tiled=True)  6.87 us
  transfers between devices with their start and end apart: 2, of which 1 were waited for; matrix products, arithmetic and copies ran while one was open for 3% of the time, Pallas kernels for 66%

profile of v2, /device:TPU:1, one launch (start us, length us, event | category | flops | bytes accessed | tf_op | source)
XLA Modules:
  0.0 146.8 jit_solution(6309999397158973541)
XLA Ops:
  7.2 0.0 copy-start
  7.2 0.0 all-gather.2.cloned.1.call-start
  7.2 0.9 copy.18
  8.1 0.6 reshape.81
  8.7 0.0 all-gather.2.cloned.1.call-update
  8.8 1.2 dynamic_slice.6
  12.0 0.0 copy-done
  12.0 0.1 copy.19
  12.1 0.1 broadcast_in_dim.185
  12.2 0.7 compare_convert_fusion
  12.9 0.8 multiply_reduce_fusion.1
  13.7 0.7 iota_reduce_fusion
  15.1 97.8 %conditional.1 = (bf16[3584,512]{1,0:T(8,128)(2,1)}) conditional(s32[]{:T(128)} %clamp.3, (s32[16]{0:T(128)}, s32[16]{0:T(128)}, s32[16,16]{1,0:T(8,128)S(1)}, bf16[1,3584,512]{2,1,0:T(8,128)(2,1)}) %tuple.130, (s32[16]{0:T(128)}, s32[16]{0:T(128)}, s32[16,16]{1,0:T(8,128)S(1)}, ...), branch_computations={%region_3.5_spmd, %region_5.7_spmd, %region_7.9_spmd, %region_9.11... | conditional | flops 752 | bytes 1224 | solution.py:165
  15.2 0.9 select_reduce_fusion.1.sources_ref
  16.0 96.6 %relocate_1_1.1 = bf16[8,2,224,512]{3,2,1,0:T(8,128)(2,1)} custom-call(s32[16]{0:T(128)S(1)} %select_reduce_fusion.1.sources_ref, bf16[8,2,224,512]{3,2,1,0:T(8,128)(2,1)} %bitcast.72), custom_call_target="tpu_custom_call" | custom-call | tf_op jit(solution)/shard_map/cond/branch_1_fun/relocate_1_1/pallas_call | solution.py:147
  112.9 0.0 all-gather.2.cloned.1.call-done.x_ref
  112.9 0.0 copy-start.1
  112.9 1.5 %copy-done.1 = bf16[256,3584]{1,0:T(8,128)(2,1)S(1)} copy-done((bf16[256,3584]{1,0:T(8,128)(2,1)S(1)}, bf16[256,3584]{1,0:T(8,128)(2,1)}, u32[]{:S(2)}) %copy-start.1) | copy-done | bytes 1835032
  114.4 0.0 copy-start.2
  114.4 0.0 copy-start.3
  114.4 0.0 copy-start.4
  114.4 8.4 %serve.1 = (bf16[3584,512]{1,0:T(8,128)(2,1)}, bf16[256,512]{1,0:T(8,128)(2,1)}) custom-call(bf16[256,3584]{1,0:T(8,128)(2,1)S(1)} %copy-done.1, bf16[3584,512]{1,0:T(8,128)(2,1)} %bitcast.70, f32[7,4,512]{2,1,0:T(4,128)S(1)} %reshape_reshape.3.s_ref, bf16[3584,512]{1,0:T(8,128)(2,1)} %get-tuple-element.674.rest_0_), custom_call_target="tpu_custom_call" | custom-call | flops 939524096 | bytes 12845056 | tf_op jit(solution)/shard_map/serve/pallas_call | solution.py:205
  122.9 6.9 %all-to-all-start = ((bf16[16,16,512]{2,1,0:T(8,128)(2,1)}), bf16[16,16,512]{2,1,0:T(8,128)(2,1)S(1)}, u32[]{:S(2)}, u32[]{:S(2)}) async-start(bf16[16,16,512]{2,1,0:T(8,128)(2,1)} %bitcast.66), calls=%async_computation | async-start | bytes 524288 | tf_op jit(solution)/shard_map/all_to_all | solution.py:244
  129.7 0.0 copy-done.2
  129.7 0.0 copy-done.3
  129.7 0.0 copy-done.4
  129.8 0.1 select_reduce_fusion.30
  129.9 0.1 copy.17
  130.0 9.3 %all-to-all-done = bf16[16,16,512]{2,1,0:T(8,128)(2,1)S(1)} async-done(((bf16[16,16,512]{2,1,0:T(8,128)(2,1)}), bf16[16,16,512]{2,1,0:T(8,128)(2,1)S(1)}, u32[]{:S(2)}, u32[]{:S(2)}) %all-to-all-start) | async-done | bytes 262176 | tf_op jit(solution)/shard_map/all_to_all | solution.py:244
  139.2 0.1 multiply_reduce_fusion
  139.4 0.6 copy.20
  (5 shorter events, 0.1 us)
Async XLA Ops:
  7.2 4.8 %copy-start = (f32[16,28,4]{1,2,0:T(4,128)S(1)}, f32[16,28,4]{1,2,0:T(4,128)}, u32[]{:S(2)}) copy-start(f32[16,28,4]{1,2,0:T(4,128)} %param.42) | copy-start | bytes 21508
  7.2 105.7 %all-gather.2.cloned.1.call-start = ((), (), s32[]{:S(2)}) async-start(), calls=%async_computation.1 | async-start | bytes 1892352 | tf_op jit(solution)/shard_map/all_gather | solution.py:241
  112.9 1.5 %copy-start.1 = (bf16[256,3584]{1,0:T(8,128)(2,1)S(1)}, bf16[256,3584]{1,0:T(8,128)(2,1)}, u32[]{:S(2)}) copy-start(bf16[256,3584]{1,0:T(8,128)(2,1)} %all-gather.2.cloned.1.call-done.x_ref) | copy-start | bytes 5505028
  114.4 15.3 %copy-start.2 = (s32[16]{0:T(128)S(1)}, s32[16]{0:T(128)}, u32[]{:S(2)}) copy-start(s32[16]{0:T(128)} %param.43) | copy-start | bytes 196
  114.4 15.3 %copy-start.3 = (f32[2,8,8]{2,1,0:T(8,128)S(1)}, f32[2,8,8]{2,1,0:T(8,128)}, u32[]{:S(2)}) copy-start(f32[2,8,8]{2,1,0:T(8,128)} %param.40) | copy-start | bytes 1540
  114.4 15.3 %copy-start.4 = (s32[2,8,8]{2,1,0:T(8,128)S(1)}, s32[2,8,8]{2,1,0:T(8,128)}, u32[]{:S(2)}) copy-start(s32[2,8,8]{2,1,0:T(8,128)} %param.39) | copy-start | bytes 1540
  122.9 16.4 %all-to-all-start = ((bf16[16,16,512]{2,1,0:T(8,128)(2,1)}), bf16[16,16,512]{2,1,0:T(8,128)(2,1)S(1)}, u32[]{:S(2)}, u32[]{:S(2)}) async-start(bf16[16,16,512]{2,1,0:T(8,128)(2,1)} %bitcast.66), calls=%async_computation | async-start | bytes 524288 | tf_op jit(solution)/shard_map/all_to_all | solution.py:244
Sparse Core Ops, SparseCore 0:
  11.5 91.9 all-gather.1
